TPU v7x, 32 devices: a whole 2x2x4 slice. The times are simulated.
32 devices in a mesh: batch: 8 (over z, y), weight: 4 (over x, core).
Axes of the slice: x: 2, y: 2, z: 4, core: 2. Of those that a mesh axis runs over, the one named last changes fastest.
Arguments:
- tokens: bfloat16 [1024, 8192], P(('batch', 'weight')), may hold values from -6 to 6
- segment_ids: int32 [1024], P('batch'), may hold values from 0 to 31, never falling along the last dimension, each value on 1 to 64 neighbouring positions
- norm_gain: float32 [8192], replicated, may hold values from 0.1 to 1.9
- query_weight: bfloat16 [8192, 8192], P('batch', 'weight'), may hold values from -0.0625 to 0.0625
- key_weight: bfloat16 [8192, 1024], P('batch'), may hold values from -0.0625 to 0.0625
- value_weight: bfloat16 [8192, 1024], P('batch'), may hold values from -0.0625 to 0.0625
Outputs:
- attended: bfloat16 [1024, 8192], P('batch', 'weight')
Inputs may be any that keep to these rules, and one draw needn't show every extreme that they name: `segment_ids`: segment ids never fall along the tokens; each id covers 1 to 64 consecutive tokens, one of them exactly 64.
All inputs are finite; a program needn't handle non-finite values.
Results may differ from a plain program's by a relative error of at most 0.0079.
Values may be sent and summed in bfloat16 or wider, within the bound.
A program may use at most 128 MiB of HBM per device.

v0:
```python
import math

import jax
import jax.numpy as jnp
from jax import lax
from jax.sharding import PartitionSpec as P

HEADS = 64
KV_HEADS = 8
HEAD_DIM = 128


ROPE_BASE = 500000.0
EPSILON = 1e-05


def positions_in_segment(seg_ids):
    places = jnp.arange(seg_ids.shape[0], dtype=jnp.int32)
    earlier = jnp.concatenate([seg_ids[:1] - 1, seg_ids[:-1]])
    starts = jnp.where(seg_ids != earlier, places, 0)
    leading = lax.cummax(starts, axis=0)
    return places - leading


def rotate(vectors, positions):
    half_dim = vectors.shape[-1] // 2
    ratios = jnp.arange(half_dim, dtype=jnp.float32) * (2.0 / vectors.shape[-1])
    frequency = jnp.exp(-math.log(ROPE_BASE) * ratios)
    angles = positions.astype(jnp.float32)[:, None] * frequency[None, :]
    cosine = jnp.cos(angles)[:, None, :]
    sine_part = jnp.sin(angles)[:, None, :]
    front_half = vectors[..., :half_dim]
    back_half = vectors[..., half_dim:]
    return jnp.concatenate(
        [front_half * cosine - back_half * sine_part, back_half * cosine + front_half * sine_part],
        axis=-1,
    )


def attend(grouped, rotated_keys, value_rows, seg_ids):
    scores = jnp.einsum(
        "ingd,jnd->ngij", grouped, rotated_keys, preferred_element_type=jnp.float32
    ) * grouped.shape[-1] ** (-0.5)
    places = jnp.arange(seg_ids.shape[0], dtype=jnp.int32)
    allowed = (seg_ids[:, None] == seg_ids[None, :]) & (places[None, :] <= places[:, None])
    weights = jnp.where(allowed, jnp.exp(scores), 0.0)
    probabilities = (weights / jnp.sum(weights, axis=-1, keepdims=True)).astype(jnp.bfloat16)
    mixed = jnp.einsum(
        "ngij,jnd->ingd", probabilities, value_rows, preferred_element_type=jnp.float32
    )
    return mixed.astype(jnp.bfloat16)


def per_device(tokens, segment_ids, norm_gain, query_weight, key_weight, value_weight):
    head_dim = HEAD_DIM
    query_cols = query_weight.shape[1]
    heads_dev = query_cols // head_dim
    group_size = HEADS // KV_HEADS
    local_kv = max(1, heads_dev // group_size)
    first_kv = lax.axis_index("weight") * heads_dev // group_size
    key_width = local_kv * head_dim
    key_block = lax.dynamic_slice_in_dim(key_weight, first_kv * head_dim, key_width, 1)
    value_block = lax.dynamic_slice_in_dim(value_weight, first_kv * head_dim, key_width, 1)
    values = tokens.astype(jnp.float32)
    inverse_rms = lax.rsqrt(jnp.mean(values * values, axis=1, keepdims=True) + EPSILON)
    normed = (values * inverse_rms * norm_gain[None, :]).astype(jnp.bfloat16)
    local_weights = jnp.concatenate([query_weight, key_block, value_block], axis=1)
    full_weights = lax.all_gather(local_weights, "batch", axis=0, tiled=True)
    projected = jnp.dot(
        lax.all_gather(normed, "weight", axis=0, tiled=True),
        full_weights,
        preferred_element_type=jnp.float32,
    )
    query_part = projected[:, :query_cols]
    key_rows = projected[:, query_cols : query_cols + key_width].astype(jnp.bfloat16)
    value_rows = projected[:, query_cols + key_width :].astype(jnp.bfloat16)
    pack_rows = projected.shape[0]
    positions = positions_in_segment(segment_ids)
    queries = rotate(query_part.reshape(pack_rows, heads_dev, head_dim), positions).astype(
        jnp.bfloat16
    )
    rotated_keys = rotate(
        key_rows.astype(jnp.float32).reshape(pack_rows, local_kv, head_dim), positions
    ).astype(jnp.bfloat16)
    grouped = queries.reshape(pack_rows, local_kv, heads_dev // local_kv, head_dim)
    attended = attend(
        grouped, rotated_keys, value_rows.reshape(pack_rows, local_kv, head_dim), segment_ids
    )
    return attended.reshape(pack_rows, query_cols)


def solution(mesh):
    placed = (
        P(("batch", "weight"), None),
        P("batch"),
        P(),
        P("batch", "weight"),
        P("batch", None),
        P("batch", None),
    )
    return jax.shard_map(
        per_device, mesh=mesh, in_specs=placed, out_specs=P("batch", "weight"), check_vma=False
    )
```

profile of v0, /device:TPU:0, one launch (start us, length us, event | category | flops | bytes accessed | tf_op | source)
XLA Modules:
  0.0 858.7 jit_solution(14576968247872091143)
XLA Ops:
  6.5 0.0 all-gather.3.cloned.1.call-start
  6.5 1.2 fusion.3
  7.8 2.0 fusion.5
  9.8 0.0 all-gather.3.cloned.1.call-update
  9.9 0.0 all-gather.5.cloned.1.call-start
  9.9 1.3 constant_dynamic-slice_fusion
  11.2 5.3 pad_maximum_fusion
  16.5 0.0 copy-start
  16.5 0.0 all-gather.5.cloned.1.call-update
  16.6 0.6 copy-done
  17.2 0.1 fusion.13
  17.3 0.1 copy.16
  17.4 0.2 reduce-window.8
  17.6 0.1 reduce
  17.7 0.1 fusion.12
  17.8 0.3 multiply_cosine_fusion
  18.1 17.2 %all-gather.3.cloned.1.call-done = bf16[128,8192]{1,0:T(8,128)(2,1)} async-done(((bf16[32,8192]{1,0:T(8,128)(2,1)}), bf16[128,8192]{1,0:T(8,128)(2,1)}) %all-gather.3.cloned.1.call-update) | async-done | bytes 2097168 | tf_op jit(solution)/shard_map/all_gather | solution.py:70
  35.3 796.6 %all-gather.5.cloned.1.call-done = bf16[8192,2560]{1,0:T(8,128)(2,1)} async-done(((bf16[1024,2560]{1,0:T(8,128)(2,1)}), bf16[8192,2560]{1,0:T(8,128)(2,1)}) %all-gather.5.cloned.1.call-update) | async-done | bytes 41943056 | tf_op jit(solution)/shard_map/all_gather | solution.py:68
  831.9 16.5 %fusion.17 = (bf16[128,2560]{1,0:T(8,128)(2,1)S(1)}, f32[128,2560]{1,0:T(8,128)S(1)}) fusion(bf16[128,8192]{1,0:T(8,128)(2,1)} %all-gather.3.cloned.1.call-done, bf16[8192,2560]{1,0:T(8,128)(2,1)} %all-gather.5.cloned.1.call-done), kind=kOutput, calls=%fused_computation.39 | convolution fusion | flops 5369036800 | bytes 46006272 | tf_op jit(solution)/shard_map/dot_general | solution.py:69
  848.4 0.1 reshape.120
  848.5 0.2 fusion.16
  848.7 0.1 slice_bitcast_fusion
  848.8 0.2 copy.29
  849.0 0.5 subtract_convert_fusion
  849.5 0.1 copy.18
  849.7 0.1 copy.19
  849.8 0.1 copy.26
  850.0 0.5 fusion.2
  850.5 0.3 convolution_convert_fusion
  850.8 1.0 copy.22
  (5 shorter events, 0.1 us)
Async XLA Ops:
  6.5 28.8 %all-gather.3.cloned.1.call-start = ((), (), s32[]{:S(2)}) async-start(), calls=%async_computation | async-start | bytes 2621440 | tf_op jit(solution)/shard_map/all_gather | solution.py:70
  9.9 822.1 %all-gather.5.cloned.1.call-start = ((), (), s32[]{:S(2)}) async-start(), calls=%async_computation.1 | async-start | bytes 47185920 | tf_op jit(solution)/shard_map/all_gather | solution.py:68
  16.5 0.7 copy-start
Sparse Core Ops, SparseCore 0:
  10.0 25.2 all-gather.2
  36.8 795.0 all-gather.4
where the time goes:
time: 859 us
  waiting for transfers between devices  814 us (95%)
  matrix products  17.3 us (2%)
  between operations  13.6 us (2%)
  other arithmetic  9.97 us (1%)
    all_gather x1, waiting for transfers between devices, per_device(): full_weights = lax.all_gather(local_weights, 'batch', axis=0, tiled=True)  797 us
  transfers between devices with their start and end apart: 2, of which 2 were waited for; matrix products, arithmetic and copies ran while one was open for 1% of the time, Pallas kernels for 0%

commit v1 on v0

--- a/solution.py
+++ b/solution.py
@@ -64,13 +64,18 @@
     values = tokens.astype(jnp.float32)
     inverse_rms = lax.rsqrt(jnp.mean(values * values, axis=1, keepdims=True) + EPSILON)
     normed = (values * inverse_rms * norm_gain[None, :]).astype(jnp.bfloat16)
+    batch_size = lax.axis_size("batch")
+    weight_size = lax.axis_size("weight")
+    own_rows = normed.shape[0]
+    slab = query_weight.shape[0]
+    mine = lax.all_to_all(normed, "batch", split_axis=1, concat_axis=0, tiled=True)
+    spread = lax.all_gather(mine, "weight", axis=0)
+    spread = spread.reshape(weight_size, batch_size, own_rows, slab).transpose(1, 0, 2, 3)
+    rows = spread.reshape(batch_size * weight_size * own_rows, slab)
     local_weights = jnp.concatenate([query_weight, key_block, value_block], axis=1)
-    full_weights = lax.all_gather(local_weights, "batch", axis=0, tiled=True)
-    projected = jnp.dot(
-        lax.all_gather(normed, "weight", axis=0, tiled=True),
-        full_weights,
-        preferred_element_type=jnp.float32,
-    )
+    partial = jnp.dot(rows, local_weights, preferred_element_type=jnp.float32).astype(jnp.bfloat16)
+    projected = lax.psum_scatter(partial, "batch", scatter_dimension=0, tiled=True)
+    projected = projected.astype(jnp.float32)
     query_part = projected[:, :query_cols]
     key_rows = projected[:, query_cols : query_cols + key_width].astype(jnp.bfloat16)
     value_rows = projected[:, query_cols + key_width :].astype(jnp.bfloat16)

time: 859 us -> 179 us (0.21)
  waiting for transfers between devices: 814 us -> 122 us
  blocking collectives: 0 us -> 21.7 us
    all_gather x2 -> x1, waiting for transfers between devices: 814 us -> 20.4 us  [per_device(): spread = lax.all_gather(mine, 'weight', axis=0)]
    reduce_scatter x0 -> x1, waiting for transfers between devices: none -> 101 us  [per_device(): lax.psum_scatter(partial, 'batch', scatter_dimension=0, tiled=True)]
    all_to_all x0 -> x1, blocking collectives: none -> 21.7 us  [per_device(): lax.all_to_all(normed, 'batch', split_axis=1, concat_axis=0, tiled=True)]
where the time goes in v1:
time: 179 us
  waiting for transfers between devices  122 us (68%)
  blocking collectives  21.7 us (12%)
  between operations  13.6 us (8%)
  matrix products  10.1 us (6%)
  other arithmetic  5.87 us (3%)
  local copies, waits for them, and re-layouts  5.72 us (3%)
    reduce_scatter x1, waiting for transfers between devices, per_device(): lax.psum_scatter(partial, 'batch', scatter_dimension=0, tiled=True)  101 us
    all_to_all x1, blocking collectives, per_device(): lax.all_to_all(normed, 'batch', split_axis=1, concat_axis=0, tiled=True)  21.7 us
    all_gather x1, waiting for transfers between devices, per_device(): spread = lax.all_gather(mine, 'weight', axis=0)  20.4 us
    dot_general x1, matrix products, per_device(): jnp.dot(rows, local_weights, preferred_element_type=jnp.float32)  9.32 us
  transfers between devices with their start and end apart: 2, of which 2 were waited for; matrix products, arithmetic and copies ran while one was open for 1% of the time, Pallas kernels for 0%

profile of v1, /device:TPU:0, one launch (start us, length us, event | category | flops | bytes accessed | tf_op | source)
XLA Modules:
  0.0 178.7 jit_solution(12772128368727349143)
XLA Ops:
  6.5 0.0 all-gather.2.cloned.1.call-start
  6.5 1.2 fusion.8
  7.8 1.2 fusion.10
  9.1 21.7 %all_to_all.16 = bf16[32,8,1024]{2,0,1:T(8,128)(2,1)} all-to-all(bf16[32,8,1024]{2,0,1:T(8,128)(2,1)S(1)} %bitcast.47), channel_id=1, replica_groups=mesh['batch'=8,'weight'=4] {'batch'}, dimensions={1} | all-to-all | bytes 1048576 | tf_op jit(solution)/shard_map/all_to_all | solution.py:71
  30.8 0.0 all-gather.2.cloned.1.call-update
  30.8 0.0 reduce-scatter.2.cloned.1.call-start
  30.9 1.3 constant_dynamic-slice_fusion
  32.2 20.4 %all-gather.2.cloned.1.call-done = bf16[4,256,1024]{2,1,0:T(8,128)(2,1)} async-done(((bf16[1,256,1024]{2,1,0:T(8,128)(2,1)}), bf16[4,256,1024]{2,1,0:T(8,128)(2,1)}) %all-gather.2.cloned.1.call-update) | async-done | bytes 2097168 | tf_op jit(solution)/shard_map/all_gather | solution.py:72
  52.6 1.8 %copy.44 = bf16[8,4,32,1024]{3,2,1,0:T(8,128)(2,1)S(1)} copy(bf16[8,4,32,1024]{3,2,0,1:T(8,128)(2,1)} %bitcast.43) | data formatting | bytes 4194304 | tf_op jit(solution)/shard_map/transpose | solution.py:73
  54.4 9.3 %convolution_convert_fusion = bf16[1024,2560]{1,0:T(8,128)(2,1)} fusion(bf16[1024,1024]{1,0:T(8,128)(2,1)S(1)} %bitcast.44, bf16[1024,256]{1,0:T(8,128)(2,1)S(1)} %get-tuple-element.15, bf16[1024,256]{1,0:T(8,128)(2,1)S(1)} %get-tuple-element.16, bf16[1024,2048]{1,0:T(8,128)(2,1)} %param.9), kind=kOutput, calls=%fused_computation | convolution fusion | flops 5387059200 | bytes 12582912 | tf_op jit(solution)/shard_map/dot_general | solution.py:76
  63.7 0.0 copy-start
  63.7 0.0 reduce-scatter.2.cloned.1.call-update
  63.7 0.6 copy-done
  64.4 0.1 fusion.18
  64.5 0.1 copy.46
  64.6 0.2 reduce-window.8
  64.8 0.1 reduce
  64.9 0.1 fusion.17
  65.0 0.3 multiply_cosine_fusion
  65.3 101.2 %reduce-scatter.2.cloned.1.call-done = bf16[128,2560]{1,0:T(8,128)(2,1)} async-done(((bf16[1024,2560]{1,0:T(8,128)(2,1)}), bf16[128,2560]{1,0:T(8,128)(2,1)}) %reduce-scatter.2.cloned.1.call-update) | async-done | bytes 655376 | tf_op jit(solution)/shard_map/reduce_scatter | solution.py:77
  166.5 0.9 slice_convert_fusion
  167.4 0.1 reshape.136
  167.4 0.2 fusion.22
  167.6 1.1 convert_bitcast_fusion
  168.8 0.2 copy.60
  169.0 0.5 subtract_convert_fusion
  169.5 0.1 copy.48
  169.7 0.1 copy.49
  169.8 0.1 copy.56
  170.0 0.5 fusion.7
  170.5 0.3 convolution_convert_fusion.1
  170.8 1.0 copy.52
  (5 shorter events, 0.1 us)
Async XLA Ops:
  6.5 46.0 %all-gather.2.cloned.1.call-start = ((), (), s32[]{:S(2)}) async-start(), calls=%async_computation.2 | async-start | bytes 2621440 | tf_op jit(solution)/shard_map/all_gather | solution.py:72
  30.8 135.6 %reduce-scatter.2.cloned.1.call-start = ((), (), s32[]{:S(2)}) async-start(), calls=%async_computation.3 | async-start | bytes 5898240 | tf_op jit(solution)/shard_map/reduce_scatter | solution.py:77
  63.7 0.7 copy-start
Sparse Core Ops, SparseCore 0:
  30.9 21.5 all-gather.1
  63.9 102.5 reduce-scatter.1

commit v2 on v0

--- a/solution.py
+++ b/solution.py
@@ -3,6 +3,8 @@
 import jax
 import jax.numpy as jnp
 from jax import lax
+from jax.experimental import pallas as pl
+from jax.experimental.pallas import tpu as pltpu
 from jax.sharding import PartitionSpec as P
 
 HEADS = 64
@@ -51,6 +53,241 @@
     return mixed.astype(jnp.bfloat16)
 
 
+MESH = pl.DeviceIdType.MESH
+TILE = 512
+
+
+def project_kernel(
+    tokens_ref, gain_ref, query_ref, key_ref, value_ref, out_ref,
+    weights, normed, rows, own, y_out, y_in, z_out, z_in,
+    load_sem, tok_send, tok_recv, x_send, core_send, relay_send,
+    y_send, y_recv, z_send, z_recv,
+):
+    me_b = lax.axis_index("batch")
+    me_w = lax.axis_index("weight")
+    z, y = me_b // 2, me_b % 2
+    count, features = tokens_ref.shape
+    slab = query_ref.shape[0]
+    pack = 4 * count
+    tiles = weights.shape[0]
+    q_tiles = tiles - 1
+    kv = TILE // 2
+
+    order = [(z + 2) % 4, 3 - z, z + 1 - 2 * (z % 2), z]
+    other_y = 1 - y
+    sources = [(zz * 2 + y, zz * 2 + other_y) for zz in order]
+    peers = [b for pair in sources for b in pair]
+    x_w, core_w, far_w = (me_w + 2) % 4, me_w + 1 - 2 * (me_w % 2), 3 - me_w
+
+    barrier = pltpu.get_barrier_semaphore()
+    for i, b in enumerate(peers):
+        if i != 6:
+            pl.semaphore_signal(barrier, inc=1, device_id=(b, me_w), device_id_type=MESH)
+    for w in (x_w, core_w):
+        pl.semaphore_signal(barrier, inc=1, device_id=(me_b, w), device_id_type=MESH)
+
+    loads = [
+        pltpu.make_async_copy(
+            query_ref.at[:, pl.ds(t * TILE, TILE)], weights.at[t], load_sem.at[t]
+        )
+        for t in range(q_tiles)
+    ]
+    first = pl.ds(pl.multiple_of(me_w * kv, kv), kv)
+    loads.append(
+        pltpu.make_async_copy(
+            key_ref.at[:, first], weights.at[q_tiles, :, pl.ds(0, kv)], load_sem.at[q_tiles]
+        )
+    )
+    loads.append(
+        pltpu.make_async_copy(
+            value_ref.at[:, first], weights.at[q_tiles, :, pl.ds(kv, kv)], load_sem.at[tiles]
+        )
+    )
+    for load in loads:
+        load.start()
+
+    total = jnp.zeros((count, 1), jnp.float32)
+    for k in range(features // slab):
+        part = tokens_ref[:, k * slab : (k + 1) * slab].astype(jnp.float32)
+        total = total + jnp.sum(part * part, axis=1, keepdims=True)
+    inverse_rms = lax.rsqrt(total * (1.0 / features) + EPSILON)
+    for k in range(features // slab):
+        part = tokens_ref[:, k * slab : (k + 1) * slab].astype(jnp.float32)
+        normed[k] = (part * inverse_rms * gain_ref[:, k * slab : (k + 1) * slab]).astype(jnp.bfloat16)
+
+    def slot(b, w):
+        return b * 4 + w
+
+    def at_slot(s):
+        return rows.at[pl.ds(pl.multiple_of(s * count, count), count)]
+
+    def send(src, s, device, send_sem):
+        return pltpu.make_async_remote_copy(
+            src_ref=src, dst_ref=at_slot(s), send_sem=send_sem, recv_sem=tok_recv.at[s],
+            device_id=device, device_id_type=MESH,
+        )
+
+    def arrived(s):
+        send(at_slot(s), s, (me_b, x_w), x_send.at[0]).wait_recv()
+
+    pl.semaphore_wait(barrier, 9)
+    mine = slot(me_b, me_w)
+    sent = []
+    for i, b in enumerate(peers):
+        if i != 6:
+            copy = send(normed.at[b], mine, (b, me_w), tok_send.at[i])
+            copy.start()
+            sent.append(copy)
+    rows[pl.ds(pl.multiple_of(mine * count, count), count), :] = normed[me_b]
+
+    def forward(i):
+        b = peers[i]
+        s = slot(b, me_w)
+        if i != 6:
+            arrived(s)
+        for w, sem in ((x_w, x_send), (core_w, core_send)):
+            copy = send(at_slot(s), s, (me_b, w), sem.at[i])
+            copy.start()
+            sent.append(copy)
+
+    def relay(i):
+        s = slot(peers[i], x_w)
+        arrived(s)
+        copy = send(at_slot(s), s, (me_b, core_w), relay_send.at[i])
+        copy.start()
+        sent.append(copy)
+
+    def collect(i):
+        arrived(slot(peers[i], core_w))
+        arrived(slot(peers[i], far_w))
+
+    own_rows = pl.ds(pl.multiple_of(y * pack, pack), pack)
+    other_rows = pl.ds(pl.multiple_of(other_y * pack, pack), pack)
+
+    def y_copy(c, t):
+        return pltpu.make_async_remote_copy(
+            src_ref=y_out.at[c, t], dst_ref=y_in.at[c, t],
+            send_sem=y_send.at[c, t], recv_sem=y_recv.at[c, t],
+            device_id=(z * 2 + other_y, me_w), device_id_type=MESH,
+        )
+
+    def z_copy(c, t):
+        return pltpu.make_async_remote_copy(
+            src_ref=z_out.at[c, t], dst_ref=z_in.at[c, t],
+            send_sem=z_send.at[c, t], recv_sem=z_recv.at[c, t],
+            device_id=(order[c] * 2 + y, me_w), device_id_type=MESH,
+        )
+
+    def multiply(c):
+        chunk = pl.ds(pl.multiple_of(order[c] * 2 * pack, 2 * pack), 2 * pack)
+
+        @pl.loop(0, tiles)
+        def _(t):
+            own[c, t] = jnp.dot(rows[chunk, :], weights[t], preferred_element_type=jnp.float32)
+            y_out[c, t] = own[c, t, other_rows, :].astype(jnp.bfloat16)
+            y_copy(c, t).start()
+
+    def pair_sum(c, t):
+        y_copy(c, t).wait_recv()
+        return own[c, t, own_rows, :] + y_in[c, t].astype(jnp.float32)
+
+    def pass_on(c):
+        @pl.loop(0, tiles)
+        def _(t):
+            z_out[c, t] = pair_sum(c, t).astype(jnp.bfloat16)
+            z_copy(c, t).start()
+
+    def bring(c):
+        for step in (forward, relay):
+            step(2 * c)
+            step(2 * c + 1)
+
+    forward(6)
+    bring(0)
+    for load in loads:
+        load.wait()
+    for c in (0, 1):
+        if c == 1:
+            bring(1)
+        collect(2 * c)
+        collect(2 * c + 1)
+        multiply(c)
+    bring(2)
+    forward(7)
+    relay(6)
+    relay(7)
+    pass_on(0)
+    collect(4)
+    collect(5)
+    multiply(2)
+    collect(6)
+    collect(7)
+    multiply(3)
+    pass_on(1)
+    pass_on(2)
+
+    @pl.loop(0, tiles)
+    def _(t):
+        result = pair_sum(3, t)
+        for c in range(3):
+            z_copy(c, t).wait_recv()
+            result = result + z_in[c, t].astype(jnp.float32)
+        out_ref[t] = result
+
+    for copy in sent:
+        copy.wait_send()
+
+    @pl.loop(0, tiles)
+    def _(t):
+        for c in range(4):
+            y_copy(c, t).wait_send()
+        for c in range(3):
+            z_copy(c, t).wait_send()
+
+
+def project_on_slice(tokens, norm_gain, query_weight, key_weight, value_weight):
+    count, features = tokens.shape
+    slab, query_cols = query_weight.shape
+    tiles = query_cols // TILE + 1
+    pack = 4 * count
+    bf16, f32 = jnp.bfloat16, jnp.float32
+    dma = pltpu.SemaphoreType.DMA
+    vmem = pl.BlockSpec(memory_space=pltpu.VMEM)
+    anywhere = pl.BlockSpec(memory_space=pl.ANY)
+    return pl.pallas_call(
+        project_kernel,
+        out_shape=jax.ShapeDtypeStruct((tiles, pack, TILE), f32),
+        in_specs=[vmem, vmem, anywhere, anywhere, anywhere],
+        out_specs=vmem,
+        scratch_shapes=[
+            pltpu.VMEM((tiles, slab, TILE), bf16),
+            pltpu.VMEM((8, count, slab), bf16),
+            pltpu.VMEM((8 * pack, slab), bf16),
+            pltpu.VMEM((4, tiles, 2 * pack, TILE), f32),
+            pltpu.VMEM((4, tiles, pack, TILE), bf16),
+            pltpu.VMEM((4, tiles, pack, TILE), bf16),
+            pltpu.VMEM((3, tiles, pack, TILE), bf16),
+            pltpu.VMEM((3, tiles, pack, TILE), bf16),
+            dma((tiles + 1,)),
+            dma((8,)),
+            dma((32,)),
+            dma((8,)),
+            dma((8,)),
+            dma((8,)),
+            dma((4, tiles)),
+            dma((4, tiles)),
+            dma((3, tiles)),
+            dma((3, tiles)),
+        ],
+        compiler_params=pltpu.CompilerParams(
+            collective_id=0, has_side_effects=True, vmem_limit_bytes=48 * 1024 * 1024
+        ),
+        cost_estimate=pl.CostEstimate(
+            flops=2 * 8 * pack * slab * tiles * TILE, bytes_accessed=2 * slab * tiles * TILE, transcendentals=0
+        ),
+    )(tokens, norm_gain[None, :], query_weight, key_weight, value_weight)
+
+
 def per_device(tokens, segment_ids, norm_gain, query_weight, key_weight, value_weight):
     head_dim = HEAD_DIM
     query_cols = query_weight.shape[1]
@@ -59,22 +296,28 @@
     local_kv = max(1, heads_dev // group_size)
     first_kv = lax.axis_index("weight") * heads_dev // group_size
     key_width = local_kv * head_dim
-    key_block = lax.dynamic_slice_in_dim(key_weight, first_kv * head_dim, key_width, 1)
-    value_block = lax.dynamic_slice_in_dim(value_weight, first_kv * head_dim, key_width, 1)
-    values = tokens.astype(jnp.float32)
-    inverse_rms = lax.rsqrt(jnp.mean(values * values, axis=1, keepdims=True) + EPSILON)
-    normed = (values * inverse_rms * norm_gain[None, :]).astype(jnp.bfloat16)
-    local_weights = jnp.concatenate([query_weight, key_block, value_block], axis=1)
-    full_weights = lax.all_gather(local_weights, "batch", axis=0, tiled=True)
-    projected = jnp.dot(
-        lax.all_gather(normed, "weight", axis=0, tiled=True),
-        full_weights,
-        preferred_element_type=jnp.float32,
-    )
-    query_part = projected[:, :query_cols]
-    key_rows = projected[:, query_cols : query_cols + key_width].astype(jnp.bfloat16)
-    value_rows = projected[:, query_cols + key_width :].astype(jnp.bfloat16)
-    pack_rows = projected.shape[0]
+    if (lax.axis_size("batch"), lax.axis_size("weight"), 2 * key_width) == (8, 4, TILE):
+        tiles = project_on_slice(tokens, norm_gain, query_weight, key_weight, value_weight)
+        query_part = tiles[:-1].transpose(1, 0, 2).reshape(tiles.shape[1], query_cols)
+        key_rows = tiles[-1, :, :key_width].astype(jnp.bfloat16)
+        value_rows = tiles[-1, :, key_width:].astype(jnp.bfloat16)
+    else:
+        key_block = lax.dynamic_slice_in_dim(key_weight, first_kv * head_dim, key_width, 1)
+        value_block = lax.dynamic_slice_in_dim(value_weight, first_kv * head_dim, key_width, 1)
+        values = tokens.astype(jnp.float32)
+        inverse_rms = lax.rsqrt(jnp.mean(values * values, axis=1, keepdims=True) + EPSILON)
+        normed = (values * inverse_rms * norm_gain[None, :]).astype(jnp.bfloat16)
+        local_weights = jnp.concatenate([query_weight, key_block, value_block], axis=1)
+        full_weights = lax.all_gather(local_weights, "batch", axis=0, tiled=True)
+        projected = jnp.dot(
+            lax.all_gather(normed, "weight", axis=0, tiled=True),
+            full_weights,
+            preferred_element_type=jnp.float32,
+        )
+        query_part = projected[:, :query_cols]
+        key_rows = projected[:, query_cols : query_cols + key_width].astype(jnp.bfloat16)
+        value_rows = projected[:, query_cols + key_width :].astype(jnp.bfloat16)
+    pack_rows = segment_ids.shape[0]
     positions = positions_in_segment(segment_ids)
     queries = rotate(query_part.reshape(pack_rows, heads_dev, head_dim), positions).astype(
         jnp.bfloat16

time: 859 us -> 102 us (0.12)
  waiting for transfers between devices: 814 us -> 0 us
  Pallas kernels: 0 us -> 89.9 us
  matrix products: 17.3 us -> 0.83 us
  between operations: 13.6 us -> 0.2 us
  other arithmetic: 9.97 us -> 0.95 us
    all_gather x2 -> x0, waiting for transfers between devices: 814 us -> none  [the longest x1 797 us: per_device(): full_weights = lax.all_gather(local_weights, 'batch', axis=0, tiled=True)]
    pallas_call x0 -> x1, Pallas kernels: none -> 89.9 us  [project_on_slice(): pl.pallas_call(project_kernel, out_shape=jax.ShapeDtypeStruct((tiles, pac...]
    dot_general x1 -> x0, matrix products: 16.5 us -> none  [per_device(): jnp.dot(lax.all_gather(normed, 'weight', axis=0, tiled=True), full_weight...]
  transfers between devices with their start and end apart: 2 -> 0, of which waited for: 2 -> 0; matrix products, arithmetic and copies ran while one was open for 1% -> 0% of each run, Pallas kernels for 0% -> 0%
where the time goes in v2:
time: 102 us; the launch traced here: 99.8 us
  Pallas kernels  89.9 us (88%)
  local copies, waits for them, and re-layouts  7.86 us (8%)
    pallas_call x1, Pallas kernels, project_on_slice(): pl.pallas_call(project_kernel, out_shape=jax.ShapeDtypeStruct((tiles, pac...  89.9 us
    unnamed x10, local copies, waits for them, and re-layouts  5.21 us

profile of v2, /device:TPU:0, one launch (start us, length us, event | category | flops | bytes accessed | tf_op | source)
XLA Modules:
  0.0 99.8 jit_solution(13497983597241612535)
XLA Ops:
  0.0 0.0 copy-start
  0.0 1.6 %copy-done = bf16[1024,1024]{1,0:T(8,128)(2,1)S(1)} copy-done((bf16[1024,1024]{1,0:T(8,128)(2,1)S(1)}, bf16[1024,1024]{1,0:T(8,128)(2,1)}, u32[]{:S(2)}) %copy-start) | copy-done | bytes 2097176
  1.6 0.0 copy-start.1
  1.6 1.6 %copy-done.1 = bf16[1024,1024]{1,0:T(8,128)(2,1)S(1)} copy-done((bf16[1024,1024]{1,0:T(8,128)(2,1)S(1)}, bf16[1024,1024]{1,0:T(8,128)(2,1)}, u32[]{:S(2)}) %copy-start.1) | copy-done | bytes 2097176
  3.2 0.0 copy-start.2
  3.2 1.0 %copy-done.2 = bf16[32,8192]{1,0:T(8,128)(2,1)S(1)} copy-done((bf16[32,8192]{1,0:T(8,128)(2,1)S(1)}, bf16[32,8192]{1,0:T(8,128)(2,1)}, u32[]{:S(2)}) %copy-start.2) | copy-done | bytes 524312
  4.2 0.0 copy-start.3
  4.2 0.8 copy-done.3
  5.0 89.9 %shard_map.64 = f32[5,128,512]{2,1,0:T(8,128)S(1)} custom-call(bf16[32,8192]{1,0:T(8,128)(2,1)S(1)} %copy-done.2, f32[1,8192]{1,0:T(1,128)S(1)} %bitcast.29, bf16[1024,2048]{1,0:T(8,128)(2,1)} %query_ref.1, bf16[1024,1024]{1,0:T(8,128)(2,1)S(1)} %copy-done, bf16[1024,1024]{1,0:T(8,128)(2,1)S(1)} %copy-done.1), custom_call_target="tpu_custom_call" | custom-call | flops 5368709120 | bytes 5242880 | tf_op jit(solution)/shard_map/pallas_call | solution.py:257
  94.9 0.1 convert.19
  95.0 0.1 copy.38
  95.1 0.0 copy-start.4
  95.2 0.1 slice_bitcast_fusion
  95.2 0.3 copy.29
  95.6 0.2 copy-done.4
  95.8 0.1 fusion.10
  95.9 0.1 copy.25
  96.0 0.2 reduce-window.8
  96.2 0.1 reduce
  96.3 0.2 multiply_cosine_fusion
  96.5 0.2 subtract_convert_fusion
  96.7 0.3 copy.31
  97.0 0.3 copy.30
  97.3 0.1 fusion.9
  97.4 0.1 reshape.102
  97.5 0.2 fusion.13
  97.7 0.1 copy.28
  97.8 0.1 copy.26
  97.9 0.5 fusion.2
  98.4 0.3 convolution_convert_fusion
  98.7 1.0 %copy.34 = bf16[128,2048]{1,0:T(8,128)(2,1)} copy(bf16[128,2048]{0,1:T(8,128)(2,1)S(1)} %bitcast.33) | data formatting | bytes 1048576 | tf_op jit(solution)/shard_map/reshape | solution.py:332
  (4 shorter events, 0.1 us)
Async XLA Ops:
  0.0 1.6 %copy-start = (bf16[1024,1024]{1,0:T(8,128)(2,1)S(1)}, bf16[1024,1024]{1,0:T(8,128)(2,1)}, u32[]{:S(2)}) copy-start(bf16[1024,1024]{1,0:T(8,128)(2,1)} %key_ref.1) | copy-start | bytes 6291460
  1.6 1.6 %copy-start.1 = (bf16[1024,1024]{1,0:T(8,128)(2,1)S(1)}, bf16[1024,1024]{1,0:T(8,128)(2,1)}, u32[]{:S(2)}) copy-start(bf16[1024,1024]{1,0:T(8,128)(2,1)} %value_ref.1) | copy-start | bytes 6291460
  3.2 1.0 %copy-start.2 = (bf16[32,8192]{1,0:T(8,128)(2,1)S(1)}, bf16[32,8192]{1,0:T(8,128)(2,1)}, u32[]{:S(2)}) copy-start(bf16[32,8192]{1,0:T(8,128)(2,1)} %tokens_ref.1) | copy-start | bytes 1572868
  4.2 0.8 copy-start.3
  95.1 0.7 copy-start.4

commit v3 on v2

--- a/solution.py
+++ b/solution.py
@@ -59,9 +59,9 @@
 
 def project_kernel(
     tokens_ref, gain_ref, query_ref, key_ref, value_ref, out_ref,
-    weights, normed, rows, own, y_out, y_in, z_out, z_in,
+    tokens, gain, weights, normed, rows, own, y_out, y_in, near_out, near_in, kv_out, kv_in, mid_out, mid_in,
     load_sem, tok_send, tok_recv, x_send, core_send, relay_send,
-    y_send, y_recv, z_send, z_recv,
+    y_send, y_recv, near_send, near_recv, kv_send, kv_recv, mid_send, mid_recv,
 ):
     me_b = lax.axis_index("batch")
     me_w = lax.axis_index("weight")
@@ -73,7 +73,8 @@
     q_tiles = tiles - 1
     kv = TILE // 2
 
-    order = [(z + 2) % 4, 3 - z, z + 1 - 2 * (z % 2), z]
+    near_z, mid_z = z + 1 - 2 * (z % 2), (z + 2) % 4
+    order = [z, 3 - z, mid_z, near_z]
     other_y = 1 - y
     sources = [(zz * 2 + y, zz * 2 + other_y) for zz in order]
     peers = [b for pair in sources for b in pair]
@@ -81,11 +82,15 @@
 
     barrier = pltpu.get_barrier_semaphore()
     for i, b in enumerate(peers):
-        if i != 6:
+        if i != 0:
             pl.semaphore_signal(barrier, inc=1, device_id=(b, me_w), device_id_type=MESH)
     for w in (x_w, core_w):
         pl.semaphore_signal(barrier, inc=1, device_id=(me_b, w), device_id_type=MESH)
 
+    token_load = pltpu.make_async_copy(tokens_ref, tokens, load_sem.at[tiles + 1])
+    gain_load = pltpu.make_async_copy(gain_ref, gain, load_sem.at[tiles + 2])
+    token_load.start()
+    gain_load.start()
     loads = [
         pltpu.make_async_copy(
             query_ref.at[:, pl.ds(t * TILE, TILE)], weights.at[t], load_sem.at[t]
@@ -106,14 +111,16 @@
     for load in loads:
         load.start()
 
+    token_load.wait()
+    gain_load.wait()
     total = jnp.zeros((count, 1), jnp.float32)
     for k in range(features // slab):
-        part = tokens_ref[:, k * slab : (k + 1) * slab].astype(jnp.float32)
+        part = tokens[:, k * slab : (k + 1) * slab].astype(jnp.float32)
         total = total + jnp.sum(part * part, axis=1, keepdims=True)
     inverse_rms = lax.rsqrt(total * (1.0 / features) + EPSILON)
     for k in range(features // slab):
-        part = tokens_ref[:, k * slab : (k + 1) * slab].astype(jnp.float32)
-        normed[k] = (part * inverse_rms * gain_ref[:, k * slab : (k + 1) * slab]).astype(jnp.bfloat16)
+        part = tokens[:, k * slab : (k + 1) * slab].astype(jnp.float32)
+        normed[k] = (part * inverse_rms * gain[:, k * slab : (k + 1) * slab]).astype(jnp.bfloat16)
 
     def slot(b, w):
         return b * 4 + w
@@ -134,7 +141,7 @@
     mine = slot(me_b, me_w)
     sent = []
     for i, b in enumerate(peers):
-        if i != 6:
+        if i != 0:
             copy = send(normed.at[b], mine, (b, me_w), tok_send.at[i])
             copy.start()
             sent.append(copy)
@@ -143,7 +150,7 @@
     def forward(i):
         b = peers[i]
         s = slot(b, me_w)
-        if i != 6:
+        if i != 0:
             arrived(s)
         for w, sem in ((x_w, x_send), (core_w, core_send)):
             copy = send(at_slot(s), s, (me_b, w), sem.at[i])
@@ -171,19 +178,44 @@
             device_id=(z * 2 + other_y, me_w), device_id_type=MESH,
         )
 
-    def z_copy(c, t):
+    def near_copy(j, t):
         return pltpu.make_async_remote_copy(
-            src_ref=z_out.at[c, t], dst_ref=z_in.at[c, t],
-            send_sem=z_send.at[c, t], recv_sem=z_recv.at[c, t],
-            device_id=(order[c] * 2 + y, me_w), device_id_type=MESH,
-        )
+            src_ref=near_out.at[j, t], dst_ref=near_in.at[j, t],
+            send_sem=near_send.at[j, t], recv_sem=near_recv.at[j, t],
+            device_id=(near_z * 2 + y, me_w), device_id_type=MESH,
+        )
+
+    def kv_copy(j):
+        return pltpu.make_async_remote_copy(
+            src_ref=kv_out.at[j], dst_ref=kv_in.at[j],
+            send_sem=kv_send.at[j], recv_sem=kv_recv.at[j],
+            device_id=(near_z * 2 + y, me_w), device_id_type=MESH,
+        )
+
+    def mid_copy(t):
+        return pltpu.make_async_remote_copy(
+            src_ref=mid_out.at[t], dst_ref=mid_in.at[t],
+            send_sem=mid_send.at[t], recv_sem=mid_recv.at[t],
+            device_id=(mid_z * 2 + y, me_w), device_id_type=MESH,
+        )
+
+    def chunk(c):
+        return pl.ds(pl.multiple_of(order[c] * 2 * pack, 2 * pack), 2 * pack)
+
+    def product(c, t):
+        return jnp.dot(rows[chunk(c), :], weights[t], preferred_element_type=jnp.float32)
+
+    def multiply_kv(c):
+        if c % 2:
+            kv_out[c // 2] = product(c, q_tiles).astype(jnp.bfloat16)
+            kv_copy(c // 2).start()
+        else:
+            own[c, q_tiles] = product(c, q_tiles)
 
     def multiply(c):
-        chunk = pl.ds(pl.multiple_of(order[c] * 2 * pack, 2 * pack), 2 * pack)
-
-        @pl.loop(0, tiles)
+        @pl.loop(0, q_tiles)
         def _(t):
-            own[c, t] = jnp.dot(rows[chunk, :], weights[t], preferred_element_type=jnp.float32)
+            own[c, t] = product(c, t)
             y_out[c, t] = own[c, t, other_rows, :].astype(jnp.bfloat16)
             y_copy(c, t).start()
 
@@ -191,58 +223,76 @@
         y_copy(c, t).wait_recv()
         return own[c, t, own_rows, :] + y_in[c, t].astype(jnp.float32)
 
-    def pass_on(c):
-        @pl.loop(0, tiles)
+    def pass_near(j):
+        @pl.loop(0, q_tiles)
         def _(t):
-            z_out[c, t] = pair_sum(c, t).astype(jnp.bfloat16)
-            z_copy(c, t).start()
-
-    def bring(c):
-        for step in (forward, relay):
+            near_out[j, t] = pair_sum(2 * j + 1, t).astype(jnp.bfloat16)
+            near_copy(j, t).start()
+
+    def ready(c):
+        for step in (forward, relay, collect):
             step(2 * c)
             step(2 * c + 1)
 
-    forward(6)
-    bring(0)
+    ready(0)
     for load in loads:
         load.wait()
-    for c in (0, 1):
-        if c == 1:
-            bring(1)
-        collect(2 * c)
-        collect(2 * c + 1)
-        multiply(c)
-    bring(2)
-    forward(7)
-    relay(6)
-    relay(7)
-    pass_on(0)
-    collect(4)
-    collect(5)
+    multiply(0)
+    ready(1)
+    multiply_kv(1)
+    multiply(1)
+    ready(2)
     multiply(2)
-    collect(6)
-    collect(7)
+    ready(3)
+    multiply_kv(3)
+    multiply_kv(2)
+    multiply_kv(0)
+    for c, j in ((2, 0), (0, 1)):
+        kv_copy(j).wait_recv()
+        own[c, q_tiles] = own[c, q_tiles] + kv_in[j].astype(jnp.float32)
+        y_out[c, q_tiles] = own[c, q_tiles, other_rows, :].astype(jnp.bfloat16)
+        y_copy(c, q_tiles).start()
     multiply(3)
-    pass_on(1)
-    pass_on(2)
-
-    @pl.loop(0, tiles)
+    pass_near(0)
+
+    @pl.loop(0, q_tiles)
     def _(t):
-        result = pair_sum(3, t)
-        for c in range(3):
-            z_copy(c, t).wait_recv()
-            result = result + z_in[c, t].astype(jnp.float32)
-        out_ref[t] = result
+        total = pair_sum(2, t)
+        near_copy(0, t).wait_recv()
+        mid_out[t] = (total + near_in[0, t].astype(jnp.float32)).astype(jnp.bfloat16)
+        mid_copy(t).start()
+
+    mid_out[q_tiles] = pair_sum(2, q_tiles).astype(jnp.bfloat16)
+    mid_copy(q_tiles).start()
+    pass_near(1)
+
+    kv_total = pair_sum(0, q_tiles)
+    mid_copy(q_tiles).wait_recv()
+    out_ref[q_tiles] = kv_total + mid_in[q_tiles].astype(jnp.float32)
+
+    @pl.loop(0, q_tiles)
+    def _(t):
+        total = pair_sum(0, t)
+        mid_copy(t).wait_recv()
+        total = total + mid_in[t].astype(jnp.float32)
+        near_copy(1, t).wait_recv()
+        out_ref[t] = total + near_in[1, t].astype(jnp.float32)
 
     for copy in sent:
         copy.wait_send()
 
-    @pl.loop(0, tiles)
+    @pl.loop(0, q_tiles)
     def _(t):
         for c in range(4):
             y_copy(c, t).wait_send()
-        for c in range(3):
-            z_copy(c, t).wait_send()
+        for j in range(2):
+            near_copy(j, t).wait_send()
+        mid_copy(t).wait_send()
+
+    for j in range(2):
+        kv_copy(j).wait_send()
+        y_copy(2 * j, q_tiles).wait_send()
+    mid_copy(q_tiles).wait_send()
 
 
 def project_on_slice(tokens, norm_gain, query_weight, key_weight, value_weight):
@@ -253,22 +303,28 @@
     bf16, f32 = jnp.bfloat16, jnp.float32
     dma = pltpu.SemaphoreType.DMA
     vmem = pl.BlockSpec(memory_space=pltpu.VMEM)
-    anywhere = pl.BlockSpec(memory_space=pl.ANY)
+    hbm = pl.BlockSpec(memory_space=pltpu.HBM)
     return pl.pallas_call(
         project_kernel,
         out_shape=jax.ShapeDtypeStruct((tiles, pack, TILE), f32),
-        in_specs=[vmem, vmem, anywhere, anywhere, anywhere],
+        in_specs=[hbm] * 5,
         out_specs=vmem,
         scratch_shapes=[
+            pltpu.VMEM((count, features), bf16),
+            pltpu.VMEM((1, features), f32),
             pltpu.VMEM((tiles, slab, TILE), bf16),
             pltpu.VMEM((8, count, slab), bf16),
             pltpu.VMEM((8 * pack, slab), bf16),
             pltpu.VMEM((4, tiles, 2 * pack, TILE), f32),
             pltpu.VMEM((4, tiles, pack, TILE), bf16),
             pltpu.VMEM((4, tiles, pack, TILE), bf16),
-            pltpu.VMEM((3, tiles, pack, TILE), bf16),
-            pltpu.VMEM((3, tiles, pack, TILE), bf16),
-            dma((tiles + 1,)),
+            pltpu.VMEM((2, tiles - 1, pack, TILE), bf16),
+            pltpu.VMEM((2, tiles - 1, pack, TILE), bf16),
+            pltpu.VMEM((2, 2 * pack, TILE), bf16),
+            pltpu.VMEM((2, 2 * pack, TILE), bf16),
+            pltpu.VMEM((tiles, pack, TILE), bf16),
+            pltpu.VMEM((tiles, pack, TILE), bf16),
+            dma((tiles + 3,)),
             dma((8,)),
             dma((32,)),
             dma((8,)),
@@ -276,11 +332,15 @@
             dma((8,)),
             dma((4, tiles)),
             dma((4, tiles)),
-            dma((3, tiles)),
-            dma((3, tiles)),
+            dma((2, tiles - 1)),
+            dma((2, tiles - 1)),
+            dma((2,)),
+            dma((2,)),
+            dma((tiles,)),
+            dma((tiles,)),
         ],
         compiler_params=pltpu.CompilerParams(
-            collective_id=0, has_side_effects=True, vmem_limit_bytes=48 * 1024 * 1024
+            collective_id=0, has_side_effects=True, vmem_limit_bytes=56 * 1024 * 1024
         ),
         cost_estimate=pl.CostEstimate(
             flops=2 * 8 * pack * slab * tiles * TILE, bytes_accessed=2 * slab * tiles * TILE, transcendentals=0

time: 102 us -> 91.7 us (0.90); the launches traced: 99.8 us -> 91.5 us
  local copies, waits for them, and re-layouts: 7.86 us -> 2.95 us
  Pallas kernels: 89.9 us -> 85.2 us
  other arithmetic: 0.95 us -> 2.37 us
    unnamed x10 -> x4, local copies, waits for them, and re-layouts: 5.21 us -> 0.29 us
    pallas_call x1, Pallas kernels: 89.9 us -> 85.2 us  [project_on_slice(): pl.pallas_call(project_kernel, out_shape=jax.ShapeDtypeStruct((tiles, pac...]
    another operation x6, other arithmetic: 0.63 us -> 2.05 us
where the time goes in v3:
time: 91.7 us; the launch traced here: 91.5 us
  Pallas kernels  85.2 us (93%)
  local copies, waits for them, and re-layouts  2.95 us (3%)
  other arithmetic  2.37 us (3%)
    pallas_call x1, Pallas kernels, project_on_slice(): pl.pallas_call(project_kernel, out_shape=jax.ShapeDtypeStruct((tiles, pac...  85.2 us
    another operation x6, other arithmetic  2.05 us

profile of v3, /device:TPU:0, one launch (start us, length us, event | category | flops | bytes accessed | tf_op | source)
XLA Modules:
  0.0 91.5 jit_solution(16903717009572823851)
XLA Ops:
  0.0 85.2 %shard_map.64 = f32[5,128,512]{2,1,0:T(8,128)} custom-call(bf16[32,8192]{1,0:T(8,128)(2,1)} %tokens_ref.1, f32[1,8192]{1,0:T(1,128)} %bitcast.36, bf16[1024,2048]{1,0:T(8,128)(2,1)} %query_ref.1, bf16[1024,1024]{1,0:T(8,128)(2,1)} %key_ref.1, bf16[1024,1024]{1,0:T(8,128)(2,1)} %value_ref.1), custom_call_target="tpu_custom_call" | custom-call | flops 5368709120 | bytes 5242880 | tf_op jit(solution)/shard_map/pallas_call | solution.py:307
  85.2 0.0 copy-start
  85.2 1.5 %convert.19 = bf16[5,128,512]{2,1,0:T(8,128)(2,1)S(1)} convert(f32[5,128,512]{2,1,0:T(8,128)} %shard_map.64) | non-fusion elementwise | flops 327680 | bytes 1966080 | tf_op jit(solution)/shard_map/convert.8
  86.8 0.1 copy.38
  86.9 0.1 copy-done
  86.9 0.0 copy-start.1
  86.9 0.1 slice_bitcast_fusion
  87.0 0.3 copy.29
  87.4 0.2 copy-done.1
  87.6 0.1 fusion.10
  87.7 0.1 copy.25
  87.8 0.2 reduce-window.8
  88.0 0.1 reduce
  88.1 0.2 multiply_cosine_fusion
  88.3 0.2 subtract_convert_fusion
  88.5 0.3 copy.31
  88.8 0.3 copy.30
  89.1 0.1 fusion.9
  89.2 0.1 reshape.102
  89.2 0.2 fusion.13
  89.4 0.1 copy.28
  89.5 0.1 copy.26
  89.7 0.5 fusion.2
  90.2 0.3 convolution_convert_fusion
  90.5 1.0 %copy.34 = bf16[128,2048]{1,0:T(8,128)(2,1)} copy(bf16[128,2048]{0,1:T(8,128)(2,1)S(1)} %bitcast.32) | data formatting | bytes 1048576 | tf_op jit(solution)/shard_map/reshape | solution.py:392
  (4 shorter events, 0.1 us)
Async XLA Ops:
  85.2 1.7 %copy-start = (f32[5,128,512]{2,1,0:T(8,128)S(1)}, f32[5,128,512]{2,1,0:T(8,128)}, u32[]{:S(2)}) copy-start(f32[5,128,512]{2,1,0:T(8,128)} %shard_map.64) | copy-start | bytes 3932164
  86.9 0.7 copy-start.1

commit v4 on v3

--- a/solution.py
+++ b/solution.py
@@ -212,59 +212,65 @@
         else:
             own[c, q_tiles] = product(c, q_tiles)
 
-    def multiply(c):
+    def multiply(c, start):
         @pl.loop(0, q_tiles)
         def _(t):
             own[c, t] = product(c, t)
             y_out[c, t] = own[c, t, other_rows, :].astype(jnp.bfloat16)
-            y_copy(c, t).start()
+            if start:
+                y_copy(c, t).start()
 
     def pair_sum(c, t):
         y_copy(c, t).wait_recv()
         return own[c, t, own_rows, :] + y_in[c, t].astype(jnp.float32)
 
-    def pass_near(j):
+    def pass_near(j, start_next):
         @pl.loop(0, q_tiles)
         def _(t):
-            near_out[j, t] = pair_sum(2 * j + 1, t).astype(jnp.bfloat16)
+            total = pair_sum(2 * j + 1, t)
+            if start_next:
+                y_copy(2, t).start()
+            near_out[j, t] = total.astype(jnp.bfloat16)
             near_copy(j, t).start()
 
-    def ready(c):
+    def ready(*chunks):
         for step in (forward, relay, collect):
-            step(2 * c)
-            step(2 * c + 1)
+            for c in chunks:
+                step(2 * c)
+                step(2 * c + 1)
 
     ready(0)
     for load in loads:
         load.wait()
-    multiply(0)
+    multiply(0, True)
     ready(1)
     multiply_kv(1)
-    multiply(1)
-    ready(2)
-    multiply(2)
-    ready(3)
+    multiply(1, True)
+    ready(2, 3)
     multiply_kv(3)
+    multiply(2, False)
     multiply_kv(2)
     multiply_kv(0)
+    pass_near(0, True)
+    multiply(3, False)
     for c, j in ((2, 0), (0, 1)):
         kv_copy(j).wait_recv()
         own[c, q_tiles] = own[c, q_tiles] + kv_in[j].astype(jnp.float32)
         y_out[c, q_tiles] = own[c, q_tiles, other_rows, :].astype(jnp.bfloat16)
-        y_copy(c, q_tiles).start()
-    multiply(3)
-    pass_near(0)
-
-    @pl.loop(0, q_tiles)
-    def _(t):
+
+    y_later = [(2, q_tiles), (0, q_tiles)] + [(3, t) for t in range(q_tiles)]
+    for t in range(q_tiles):
         total = pair_sum(2, t)
+        y_copy(*y_later[t]).start()
         near_copy(0, t).wait_recv()
         mid_out[t] = (total + near_in[0, t].astype(jnp.float32)).astype(jnp.bfloat16)
         mid_copy(t).start()
 
     mid_out[q_tiles] = pair_sum(2, q_tiles).astype(jnp.bfloat16)
     mid_copy(q_tiles).start()
-    pass_near(1)
+    for later in y_later[q_tiles:]:
+        y_copy(*later).start()
+    pass_near(1, False)
 
     kv_total = pair_sum(0, q_tiles)
     mid_copy(q_tiles).wait_recv()

time: 91.7 us -> 88.2 us (0.962)
  Pallas kernels: 85.2 us -> 81.7 us
    pallas_call x1, Pallas kernels: 85.2 us -> 81.7 us  [project_on_slice(): pl.pallas_call(project_kernel, out_shape=jax.ShapeDtypeStruct((tiles, pac...]
where the time goes in v4:
time: 88.2 us; the launch traced here: 88 us
  Pallas kernels  81.7 us (93%)
  local copies, waits for them, and re-layouts  2.95 us (3%)
  other arithmetic  2.37 us (3%)
    pallas_call x1, Pallas kernels, project_on_slice(): pl.pallas_call(project_kernel, out_shape=jax.ShapeDtypeStruct((tiles, pac...  81.7 us
    another operation x6, other arithmetic  2.05 us

profile of v4, /device:TPU:0, one launch (start us, length us, event | category | flops | bytes accessed | tf_op | source)
XLA Modules:
  0.0 88.0 jit_solution(8631623072888058511)
XLA Ops:
  0.0 81.7 %shard_map.64 = f32[5,128,512]{2,1,0:T(8,128)} custom-call(bf16[32,8192]{1,0:T(8,128)(2,1)} %tokens_ref.1, f32[1,8192]{1,0:T(1,128)} %bitcast.36, bf16[1024,2048]{1,0:T(8,128)(2,1)} %query_ref.1, bf16[1024,1024]{1,0:T(8,128)(2,1)} %key_ref.1, bf16[1024,1024]{1,0:T(8,128)(2,1)} %value_ref.1), custom_call_target="tpu_custom_call" | custom-call | flops 5368709120 | bytes 5242880 | tf_op jit(solution)/shard_map/pallas_call | solution.py:313
  81.7 0.0 copy-start
  81.7 1.5 %convert.19 = bf16[5,128,512]{2,1,0:T(8,128)(2,1)S(1)} convert(f32[5,128,512]{2,1,0:T(8,128)} %shard_map.64) | non-fusion elementwise | flops 327680 | bytes 1966080 | tf_op jit(solution)/shard_map/convert.8
  83.2 0.1 copy.38
  83.4 0.1 copy-done
  83.4 0.0 copy-start.1
  83.4 0.1 slice_bitcast_fusion
  83.5 0.3 copy.29
  83.8 0.2 copy-done.1
  84.1 0.1 fusion.10
  84.2 0.1 copy.25
  84.3 0.2 reduce-window.8
  84.5 0.1 reduce
  84.6 0.2 multiply_cosine_fusion
  84.8 0.2 subtract_convert_fusion
  85.0 0.3 copy.31
  85.3 0.3 copy.30
  85.6 0.1 fusion.9
  85.6 0.1 reshape.102
  85.7 0.2 fusion.13
  85.9 0.1 copy.28
  86.0 0.1 copy.26
  86.2 0.5 fusion.2
  86.7 0.3 convolution_convert_fusion
  87.0 1.0 %copy.34 = bf16[128,2048]{1,0:T(8,128)(2,1)} copy(bf16[128,2048]{0,1:T(8,128)(2,1)S(1)} %bitcast.32) | data formatting | bytes 1048576 | tf_op jit(solution)/shard_map/reshape | solution.py:398
  (4 shorter events, 0.1 us)
Async XLA Ops:
  81.7 1.7 %copy-start = (f32[5,128,512]{2,1,0:T(8,128)S(1)}, f32[5,128,512]{2,1,0:T(8,128)}, u32[]{:S(2)}) copy-start(f32[5,128,512]{2,1,0:T(8,128)} %shard_map.64) | copy-start | bytes 3932164
  83.4 0.7 copy-start.1

commit v5 on v4

--- a/solution.py
+++ b/solution.py
@@ -24,13 +24,17 @@
     return places - leading
 
 
+def rope_tables(positions, head_dim):
+    ratios = jnp.arange(head_dim // 2, dtype=jnp.float32) * (2.0 / head_dim)
+    frequency = jnp.exp(-math.log(ROPE_BASE) * ratios)
+    angles = positions.astype(jnp.float32)[:, None] * frequency[None, :]
+    return jnp.cos(angles), jnp.sin(angles)
+
+
 def rotate(vectors, positions):
     half_dim = vectors.shape[-1] // 2
-    ratios = jnp.arange(half_dim, dtype=jnp.float32) * (2.0 / vectors.shape[-1])
-    frequency = jnp.exp(-math.log(ROPE_BASE) * ratios)
-    angles = positions.astype(jnp.float32)[:, None] * frequency[None, :]
-    cosine = jnp.cos(angles)[:, None, :]
-    sine_part = jnp.sin(angles)[:, None, :]
+    cosine, sine_part = rope_tables(positions, vectors.shape[-1])
+    cosine, sine_part = cosine[:, None, :], sine_part[:, None, :]
     front_half = vectors[..., :half_dim]
     back_half = vectors[..., half_dim:]
     return jnp.concatenate(
@@ -57,9 +61,9 @@
 TILE = 512
 
 
-def project_kernel(
-    tokens_ref, gain_ref, query_ref, key_ref, value_ref, out_ref,
-    tokens, gain, weights, normed, rows, own, y_out, y_in, near_out, near_in, kv_out, kv_in, mid_out, mid_in,
+def attend_kernel(
+    tokens_ref, gain_ref, query_ref, key_ref, value_ref, cosine_ref, sine_ref, seg_col_ref, seg_row_ref, out_ref,
+    tokens, gain, weights, normed, rows, own, y_out, y_in, near_out, near_in, kv_out, kv_in, mid_out, mid_in, held_keys, held_values,
     load_sem, tok_send, tok_recv, x_send, core_send, relay_send,
     y_send, y_recv, near_send, near_recv, kv_send, kv_recv, mid_send, mid_recv,
 ):
@@ -272,9 +276,22 @@
         y_copy(*later).start()
     pass_near(1, False)
 
+    def rope(head):
+        return head * cosine_ref[...] + pltpu.roll(head, HEAD_DIM // 2, 1) * sine_ref[...]
+
     kv_total = pair_sum(0, q_tiles)
     mid_copy(q_tiles).wait_recv()
-    out_ref[q_tiles] = kv_total + mid_in[q_tiles].astype(jnp.float32)
+    kv_total = (kv_total + mid_in[q_tiles].astype(jnp.float32)).astype(jnp.bfloat16)
+    kv_heads = kv // HEAD_DIM
+    for h in range(kv_heads):
+        first_col = h * HEAD_DIM
+        key_head = kv_total[:, first_col : first_col + HEAD_DIM].astype(jnp.float32)
+        held_keys[h] = rope(key_head).astype(jnp.bfloat16)
+        held_values[h] = kv_total[:, kv + first_col : kv + first_col + HEAD_DIM]
+
+    places_i = lax.broadcasted_iota(jnp.int32, (pack, pack), 0)
+    places_j = lax.broadcasted_iota(jnp.int32, (pack, pack), 1)
+    allowed = (seg_col_ref[...] == seg_row_ref[...]) & (places_j <= places_i)
 
     @pl.loop(0, q_tiles)
     def _(t):
@@ -282,7 +299,22 @@
         mid_copy(t).wait_recv()
         total = total + mid_in[t].astype(jnp.float32)
         near_copy(1, t).wait_recv()
-        out_ref[t] = total + near_in[1, t].astype(jnp.float32)
+        total = total + near_in[1, t].astype(jnp.float32)
+        kv_head = t * kv_heads // q_tiles
+        keys, values = held_keys[kv_head], held_values[kv_head]
+        mixed = []
+        for h in range(TILE // HEAD_DIM):
+            head = rope(total[:, h * HEAD_DIM : (h + 1) * HEAD_DIM]).astype(jnp.bfloat16)
+            scores = lax.dot_general(
+                head, keys, (((1,), (1,)), ((), ())), preferred_element_type=jnp.float32
+            ) * HEAD_DIM ** (-0.5)
+            chances = jnp.where(allowed, jnp.exp(scores), 0.0)
+            chances = chances * (1.0 / jnp.sum(chances, axis=1, keepdims=True))
+            mixed.append(
+                jnp.dot(chances.astype(jnp.bfloat16), values, preferred_element_type=jnp.float32)
+            )
+        columns = pl.ds(pl.multiple_of(t * TILE, TILE), TILE)
+        out_ref[:, columns] = jnp.concatenate(mixed, axis=1).astype(jnp.bfloat16)
 
     for copy in sent:
         copy.wait_send()
@@ -301,19 +333,20 @@
     mid_copy(q_tiles).wait_send()
 
 
-def project_on_slice(tokens, norm_gain, query_weight, key_weight, value_weight):
+def attend_on_slice(tokens, segment_ids, norm_gain, query_weight, key_weight, value_weight):
     count, features = tokens.shape
     slab, query_cols = query_weight.shape
     tiles = query_cols // TILE + 1
     pack = 4 * count
+    cosine, sine_part = rope_tables(positions_in_segment(segment_ids), HEAD_DIM)
     bf16, f32 = jnp.bfloat16, jnp.float32
     dma = pltpu.SemaphoreType.DMA
     vmem = pl.BlockSpec(memory_space=pltpu.VMEM)
     hbm = pl.BlockSpec(memory_space=pltpu.HBM)
     return pl.pallas_call(
-        project_kernel,
-        out_shape=jax.ShapeDtypeStruct((tiles, pack, TILE), f32),
-        in_specs=[hbm] * 5,
+        attend_kernel,
+        out_shape=jax.ShapeDtypeStruct((pack, query_cols), bf16),
+        in_specs=[hbm] * 5 + [vmem] * 4,
         out_specs=vmem,
         scratch_shapes=[
             pltpu.VMEM((count, features), bf16),
@@ -330,6 +363,8 @@
             pltpu.VMEM((2, 2 * pack, TILE), bf16),
             pltpu.VMEM((tiles, pack, TILE), bf16),
             pltpu.VMEM((tiles, pack, TILE), bf16),
+            pltpu.VMEM((TILE // 2 // HEAD_DIM, pack, HEAD_DIM), bf16),
+            pltpu.VMEM((TILE // 2 // HEAD_DIM, pack, HEAD_DIM), bf16),
             dma((tiles + 3,)),
             dma((8,)),
             dma((32,)),
@@ -351,7 +386,11 @@
         cost_estimate=pl.CostEstimate(
             flops=2 * 8 * pack * slab * tiles * TILE, bytes_accessed=2 * slab * tiles * TILE, transcendentals=0
         ),
-    )(tokens, norm_gain[None, :], query_weight, key_weight, value_weight)
+    )(
+        tokens, norm_gain[None, :], query_weight, key_weight, value_weight,
+        jnp.concatenate([cosine, cosine], axis=1), jnp.concatenate([-sine_part, sine_part], axis=1),
+        segment_ids[:, None], segment_ids[None, :],
+    )
 
 
 def per_device(tokens, segment_ids, norm_gain, query_weight, key_weight, value_weight):
@@ -363,26 +402,22 @@
     first_kv = lax.axis_index("weight") * heads_dev // group_size
     key_width = local_kv * head_dim
     if (lax.axis_size("batch"), lax.axis_size("weight"), 2 * key_width) == (8, 4, TILE):
-        tiles = project_on_slice(tokens, norm_gain, query_weight, key_weight, value_weight)
-        query_part = tiles[:-1].transpose(1, 0, 2).reshape(tiles.shape[1], query_cols)
-        key_rows = tiles[-1, :, :key_width].astype(jnp.bfloat16)
-        value_rows = tiles[-1, :, key_width:].astype(jnp.bfloat16)
-    else:
-        key_block = lax.dynamic_slice_in_dim(key_weight, first_kv * head_dim, key_width, 1)
-        value_block = lax.dynamic_slice_in_dim(value_weight, first_kv * head_dim, key_width, 1)
-        values = tokens.astype(jnp.float32)
-        inverse_rms = lax.rsqrt(jnp.mean(values * values, axis=1, keepdims=True) + EPSILON)
-        normed = (values * inverse_rms * norm_gain[None, :]).astype(jnp.bfloat16)
-        local_weights = jnp.concatenate([query_weight, key_block, value_block], axis=1)
-        full_weights = lax.all_gather(local_weights, "batch", axis=0, tiled=True)
-        projected = jnp.dot(
-            lax.all_gather(normed, "weight", axis=0, tiled=True),
-            full_weights,
-            preferred_element_type=jnp.float32,
-        )
-        query_part = projected[:, :query_cols]
-        key_rows = projected[:, query_cols : query_cols + key_width].astype(jnp.bfloat16)
-        value_rows = projected[:, query_cols + key_width :].astype(jnp.bfloat16)
+        return attend_on_slice(tokens, segment_ids, norm_gain, query_weight, key_weight, value_weight)
+    key_block = lax.dynamic_slice_in_dim(key_weight, first_kv * head_dim, key_width, 1)
+    value_block = lax.dynamic_slice_in_dim(value_weight, first_kv * head_dim, key_width, 1)
+    values = tokens.astype(jnp.float32)
+    inverse_rms = lax.rsqrt(jnp.mean(values * values, axis=1, keepdims=True) + EPSILON)
+    normed = (values * inverse_rms * norm_gain[None, :]).astype(jnp.bfloat16)
+    local_weights = jnp.concatenate([query_weight, key_block, value_block], axis=1)
+    full_weights = lax.all_gather(local_weights, "batch", axis=0, tiled=True)
+    projected = jnp.dot(
+        lax.all_gather(normed, "weight", axis=0, tiled=True),
+        full_weights,
+        preferred_element_type=jnp.float32,
+    )
+    query_part = projected[:, :query_cols]
+    key_rows = projected[:, query_cols : query_cols + key_width].astype(jnp.bfloat16)
+    value_rows = projected[:, query_cols + key_width :].astype(jnp.bfloat16)
     pack_rows = segment_ids.shape[0]
     positions = positions_in_segment(segment_ids)
     queries = rotate(query_part.reshape(pack_rows, heads_dev, head_dim), positions).astype(

time: 88.2 us -> 89.9 us (1.019)
  Pallas kernels: 81.7 us -> 83.5 us
    pallas_call x1, Pallas kernels: 81.7 us -> 83.5 us  [attend_on_slice(): pl.pallas_call(attend_kernel, out_shape=jax.ShapeDtypeStruct((pack, query...]
    unnamed x4 -> x1, local copies, waits for them, and re-layouts: 0.29 us -> 1.88 us
    broadcast_in_dim x0 -> x1, local copies, waits for them, and re-layouts: none -> 1.38 us  [attend_on_slice(): segment_ids[:, None]]
    reshape x1 -> x0, local copies, waits for them, and re-layouts: 1.01 us -> none  [per_device(): return attended.reshape(pack_rows, query_cols)]
    another operation x6 -> x3, other arithmetic: 2.05 us -> 1.08 us
where the time goes in v5:
time: 89.9 us; the launch traced here: 89.7 us
  Pallas kernels  83.5 us (93%)
  local copies, waits for them, and re-layouts  3.38 us (4%)
  other arithmetic  2.15 us (2%)
    pallas_call x1, Pallas kernels, attend_on_slice(): pl.pallas_call(attend_kernel, out_shape=jax.ShapeDtypeStruct((pack, query...  83.5 us
    unnamed x1, local copies, waits for them, and re-layouts  1.88 us

profile of v5, /device:TPU:0, one launch (start us, length us, event | category | flops | bytes accessed | tf_op | source)
XLA Modules:
  0.0 89.7 jit_solution(14940348217724068627)
XLA Ops:
  0.7 0.8 fusion.1
  1.5 0.1 copy.9
  1.6 0.2 reduce-window.8
  1.8 0.1 reduce
  1.9 1.4 %copy.10.seg_col_ref = s32[128,1]{1,0:T(8,128)} copy(s32[128,1]{0,1:T(1,128)} %bitcast.9) | data formatting | bytes 1024 | tf_op jit(solution)/shard_map/broadcast_in_dim | solution.py:392
  3.3 0.3 fusion
  3.6 0.7 pad_maximum_fusion
  4.3 83.5 %shard_map.64 = bf16[128,2048]{1,0:T(8,128)(2,1)} custom-call(bf16[32,8192]{1,0:T(8,128)(2,1)} %tokens_ref.1, f32[1,8192]{1,0:T(1,128)} %bitcast.11, bf16[1024,2048]{1,0:T(8,128)(2,1)} %query_ref.1, bf16[1024,1024]{1,0:T(8,128)(2,1)} %key_ref.1, bf16[1024,1024]{1,0:T(8,128)(2,1)} %value_ref.1, f32[128,128]{1,0:T(8,128)} %get-tuple-element.8.cosine_ref, ...), custom_call_target="tpu_custom_call" | custom-call | flops 5368709120 | bytes 5242880 | tf_op jit(solution)/shard_map/pallas_call | solution.py:346
  87.8 1.9 %copy.12 = bf16[128,2048]{1,0:T(8,128)(2,1)} copy(bf16[128,2048]{1,0:T(8,128)(2,1)} %shard_map.64) | data formatting | bytes 1048576
  (2 shorter events, 0.0 us)

commit v6 on v5

--- a/solution.py
+++ b/solution.py
@@ -62,8 +62,8 @@
 
 
 def attend_kernel(
-    tokens_ref, gain_ref, query_ref, key_ref, value_ref, cosine_ref, sine_ref, seg_col_ref, seg_row_ref, out_ref,
-    tokens, gain, weights, normed, rows, own, y_out, y_in, near_out, near_in, kv_out, kv_in, mid_out, mid_in, held_keys, held_values,
+    tokens_ref, gain_ref, query_ref, key_ref, value_ref, seg_ref, out_ref,
+    tokens, gain, weights, normed, rows, own, y_out, y_in, near_out, near_in, kv_out, kv_in, mid_out, mid_in, held_keys, held_values, cosine, sine, allowed,
     load_sem, tok_send, tok_recv, x_send, core_send, relay_send,
     y_send, y_recv, near_send, near_recv, kv_send, kv_recv, mid_send, mid_recv,
 ):
@@ -216,8 +216,24 @@
         else:
             own[c, q_tiles] = product(c, q_tiles)
 
-    def multiply(c, start):
-        @pl.loop(0, q_tiles)
+    def make_tables():
+        places_i = lax.broadcasted_iota(jnp.int32, (pack, pack), 0)
+        places_j = lax.broadcasted_iota(jnp.int32, (pack, pack), 1)
+        seg_j = jnp.broadcast_to(seg_ref[...], (pack, pack))
+        same = seg_j.T == seg_j
+        allowed[...] = jnp.where(same & (places_j <= places_i), 1.0, 0.0)
+        start = jnp.min(jnp.where(same, places_j, pack).astype(jnp.float32), axis=1, keepdims=True)
+        shape = (pack, HEAD_DIM)
+        position = lax.broadcasted_iota(jnp.int32, shape, 0).astype(jnp.float32) - start
+        lane = lax.broadcasted_iota(jnp.int32, shape, 1)
+        half_dim = HEAD_DIM // 2
+        ratio = (lane % half_dim).astype(jnp.float32) * (2.0 / HEAD_DIM)
+        angles = position * jnp.exp(-math.log(ROPE_BASE) * ratio)
+        cosine[...] = jnp.cos(angles)
+        sine[...] = jnp.where(lane < half_dim, -1.0, 1.0) * jnp.sin(angles)
+
+    def multiply(c, start, first_tile=0, last_tile=q_tiles):
+        @pl.loop(first_tile, last_tile)
         def _(t):
             own[c, t] = product(c, t)
             y_out[c, t] = own[c, t, other_rows, :].astype(jnp.bfloat16)
@@ -228,12 +244,11 @@
         y_copy(c, t).wait_recv()
         return own[c, t, own_rows, :] + y_in[c, t].astype(jnp.float32)
 
-    def pass_near(j, start_next):
-        @pl.loop(0, q_tiles)
-        def _(t):
+    def pass_near(j, y_next):
+        for t in range(q_tiles):
             total = pair_sum(2 * j + 1, t)
-            if start_next:
-                y_copy(2, t).start()
+            if t < len(y_next):
+                y_copy(*y_next[t]).start()
             near_out[j, t] = total.astype(jnp.bfloat16)
             near_copy(j, t).start()
 
@@ -246,17 +261,19 @@
     ready(0)
     for load in loads:
         load.wait()
-    multiply(0, True)
+    multiply(0, True, 0, q_tiles - 1)
     ready(1)
+    multiply(1, True)
     multiply_kv(1)
-    multiply(1, True)
     ready(2, 3)
     multiply_kv(3)
     multiply(2, False)
     multiply_kv(2)
     multiply_kv(0)
-    pass_near(0, True)
+    make_tables()
+    pass_near(0, [(2, t) for t in range(q_tiles)])
     multiply(3, False)
+    multiply(0, False, q_tiles - 1)
     for c, j in ((2, 0), (0, 1)):
         kv_copy(j).wait_recv()
         own[c, q_tiles] = own[c, q_tiles] + kv_in[j].astype(jnp.float32)
@@ -274,10 +291,10 @@
     mid_copy(q_tiles).start()
     for later in y_later[q_tiles:]:
         y_copy(*later).start()
-    pass_near(1, False)
+    pass_near(1, [(0, q_tiles - 1)])
 
     def rope(head):
-        return head * cosine_ref[...] + pltpu.roll(head, HEAD_DIM // 2, 1) * sine_ref[...]
+        return head * cosine[...] + pltpu.roll(head, HEAD_DIM // 2, 1) * sine[...]
 
     kv_total = pair_sum(0, q_tiles)
     mid_copy(q_tiles).wait_recv()
@@ -288,10 +305,6 @@
         key_head = kv_total[:, first_col : first_col + HEAD_DIM].astype(jnp.float32)
         held_keys[h] = rope(key_head).astype(jnp.bfloat16)
         held_values[h] = kv_total[:, kv + first_col : kv + first_col + HEAD_DIM]
-
-    places_i = lax.broadcasted_iota(jnp.int32, (pack, pack), 0)
-    places_j = lax.broadcasted_iota(jnp.int32, (pack, pack), 1)
-    allowed = (seg_col_ref[...] == seg_row_ref[...]) & (places_j <= places_i)
 
     @pl.loop(0, q_tiles)
     def _(t):
@@ -308,7 +321,7 @@
             scores = lax.dot_general(
                 head, keys, (((1,), (1,)), ((), ())), preferred_element_type=jnp.float32
             ) * HEAD_DIM ** (-0.5)
-            chances = jnp.where(allowed, jnp.exp(scores), 0.0)
+            chances = jnp.where(allowed[...] > 0.0, jnp.exp(scores), 0.0)
             chances = chances * (1.0 / jnp.sum(chances, axis=1, keepdims=True))
             mixed.append(
                 jnp.dot(chances.astype(jnp.bfloat16), values, preferred_element_type=jnp.float32)
@@ -338,7 +351,6 @@
     slab, query_cols = query_weight.shape
     tiles = query_cols // TILE + 1
     pack = 4 * count
-    cosine, sine_part = rope_tables(positions_in_segment(segment_ids), HEAD_DIM)
     bf16, f32 = jnp.bfloat16, jnp.float32
     dma = pltpu.SemaphoreType.DMA
     vmem = pl.BlockSpec(memory_space=pltpu.VMEM)
@@ -346,7 +358,7 @@
     return pl.pallas_call(
         attend_kernel,
         out_shape=jax.ShapeDtypeStruct((pack, query_cols), bf16),
-        in_specs=[hbm] * 5 + [vmem] * 4,
+        in_specs=[hbm] * 5 + [vmem],
         out_specs=vmem,
         scratch_shapes=[
             pltpu.VMEM((count, features), bf16),
@@ -365,6 +377,9 @@
             pltpu.VMEM((tiles, pack, TILE), bf16),
             pltpu.VMEM((TILE // 2 // HEAD_DIM, pack, HEAD_DIM), bf16),
             pltpu.VMEM((TILE // 2 // HEAD_DIM, pack, HEAD_DIM), bf16),
+            pltpu.VMEM((pack, HEAD_DIM), f32),
+            pltpu.VMEM((pack, HEAD_DIM), f32),
+            pltpu.VMEM((pack, pack), f32),
             dma((tiles + 3,)),
             dma((8,)),
             dma((32,)),
@@ -381,15 +396,14 @@
             dma((tiles,)),
         ],
         compiler_params=pltpu.CompilerParams(
-            collective_id=0, has_side_effects=True, vmem_limit_bytes=56 * 1024 * 1024
+            collective_id=0, has_side_effects=True, vmem_limit_bytes=53 * 1024 * 1024
         ),
         cost_estimate=pl.CostEstimate(
             flops=2 * 8 * pack * slab * tiles * TILE, bytes_accessed=2 * slab * tiles * TILE, transcendentals=0
         ),
     )(
         tokens, norm_gain[None, :], query_weight, key_weight, value_weight,
-        jnp.concatenate([cosine, cosine], axis=1), jnp.concatenate([-sine_part, sine_part], axis=1),
-        segment_ids[:, None], segment_ids[None, :],
+        segment_ids[None, :],
     )
 
 

time: 89.9 us -> 80.8 us (0.90)
  Pallas kernels: 83.5 us -> 78.4 us
  other arithmetic: 2.15 us -> 0 us
  local copies, waits for them, and re-layouts: 3.38 us -> 2.21 us
    pallas_call x1, Pallas kernels: 83.5 us -> 78.4 us  [attend_on_slice(): pl.pallas_call(attend_kernel, out_shape=jax.ShapeDtypeStruct((pack, query...]
    broadcast_in_dim x1 -> x0, local copies, waits for them, and re-layouts: 1.38 us -> none  [attend_on_slice(): segment_ids[:, None]]
    another operation x3 -> x0, other arithmetic: 1.08 us -> none
    unnamed x1 -> x5, local copies, waits for them, and re-layouts: 1.88 us -> 2.21 us
where the time goes in v6:
time: 80.8 us; the launch traced here: 80.6 us
  Pallas kernels  78.4 us (97%)
  local copies, waits for them, and re-layouts  2.21 us (3%)
    pallas_call x1, Pallas kernels, attend_on_slice(): pl.pallas_call(attend_kernel, out_shape=jax.ShapeDtypeStruct((pack, query...  78.4 us
    unnamed x5, local copies, waits for them, and re-layouts  2.21 us

profile of v6, /device:TPU:0, one launch (start us, length us, event | category | flops | bytes accessed | tf_op | source)
XLA Modules:
  0.0 80.6 jit_solution(2637249856615484265)
XLA Ops:
  0.0 0.0 copy-start
  0.0 0.8 copy-done
  0.8 0.0 copy-start.1
  0.8 0.7 copy-done.1
  1.4 78.4 %shard_map.64 = bf16[128,2048]{1,0:T(8,128)(2,1)S(1)} custom-call(bf16[32,8192]{1,0:T(8,128)(2,1)} %tokens_ref.1, f32[1,8192]{1,0:T(1,128)S(1)} %bitcast.2, bf16[1024,2048]{1,0:T(8,128)(2,1)} %query_ref.1, bf16[1024,1024]{1,0:T(8,128)(2,1)} %key_ref.1, bf16[1024,1024]{1,0:T(8,128)(2,1)} %value_ref.1, s32[1,128]{1,0:T(1,128)S(1)} %bitcast.3), custom_call_target="tpu_custom_call" | custom-call | flops 5368709120 | bytes 5242880 | tf_op jit(solution)/shard_map/pallas_call | solution.py:358
  79.8 0.8 copy.8
Async XLA Ops:
  0.0 0.8 copy-start
  0.8 0.7 copy-start.1

commit v7 on v6

--- a/solution.py
+++ b/solution.py
@@ -266,12 +266,12 @@
     multiply(1, True)
     multiply_kv(1)
     ready(2, 3)
+    multiply(2, True, 0, q_tiles // 2)
     multiply_kv(3)
-    multiply(2, False)
+    multiply(2, False, q_tiles // 2)
+    pass_near(0, [(2, t) for t in range(q_tiles // 2, q_tiles)])
     multiply_kv(2)
     multiply_kv(0)
-    make_tables()
-    pass_near(0, [(2, t) for t in range(q_tiles)])
     multiply(3, False)
     multiply(0, False, q_tiles - 1)
     for c, j in ((2, 0), (0, 1)):
@@ -279,6 +279,7 @@
         own[c, q_tiles] = own[c, q_tiles] + kv_in[j].astype(jnp.float32)
         y_out[c, q_tiles] = own[c, q_tiles, other_rows, :].astype(jnp.bfloat16)
 
+    make_tables()
     y_later = [(2, q_tiles), (0, q_tiles)] + [(3, t) for t in range(q_tiles)]
     for t in range(q_tiles):
         total = pair_sum(2, t)

time: 80.8 us -> 81.7 us (1.011)
  Pallas kernels: 78.4 us -> 79.3 us
    pallas_call x1, Pallas kernels: 78.4 us -> 79.3 us  [attend_on_slice(): pl.pallas_call(attend_kernel, out_shape=jax.ShapeDtypeStruct((pack, query...]
where the time goes in v7:
time: 81.7 us; the launch traced here: 81.5 us
  Pallas kernels  79.3 us (97%)
  local copies, waits for them, and re-layouts  2.21 us (3%)
    pallas_call x1, Pallas kernels, attend_on_slice(): pl.pallas_call(attend_kernel, out_shape=jax.ShapeDtypeStruct((pack, query...  79.3 us
    unnamed x5, local copies, waits for them, and re-layouts  2.21 us

profile of v7, /device:TPU:0, one launch (start us, length us, event | category | flops | bytes accessed | tf_op | source)
XLA Modules:
  0.0 81.5 jit_solution(11564969060192812021)
XLA Ops:
  0.0 0.0 copy-start
  0.0 0.8 copy-done
  0.8 0.0 copy-start.1
  0.8 0.7 copy-done.1
  1.4 79.3 %shard_map.64 = bf16[128,2048]{1,0:T(8,128)(2,1)S(1)} custom-call(bf16[32,8192]{1,0:T(8,128)(2,1)} %tokens_ref.1, f32[1,8192]{1,0:T(1,128)S(1)} %bitcast.2, bf16[1024,2048]{1,0:T(8,128)(2,1)} %query_ref.1, bf16[1024,1024]{1,0:T(8,128)(2,1)} %key_ref.1, bf16[1024,1024]{1,0:T(8,128)(2,1)} %value_ref.1, s32[1,128]{1,0:T(1,128)S(1)} %bitcast.3), custom_call_target="tpu_custom_call" | custom-call | flops 5368709120 | bytes 5242880 | tf_op jit(solution)/shard_map/pallas_call | solution.py:359
  80.7 0.8 copy.8
Async XLA Ops:
  0.0 0.8 copy-start
  0.8 0.7 copy-start.1

commit v8 on v6

--- a/solution.py
+++ b/solution.py
@@ -252,33 +252,37 @@
             near_out[j, t] = total.astype(jnp.bfloat16)
             near_copy(j, t).start()
 
-    def ready(*chunks):
-        for step in (forward, relay, collect):
-            for c in chunks:
-                step(2 * c)
-                step(2 * c + 1)
-
-    ready(0)
+    def run(step, *chunks):
+        for c in chunks:
+            step(2 * c)
+            step(2 * c + 1)
+
+    run(forward, 0, 1)
+    run(relay, 0)
+    run(collect, 0)
     for load in loads:
         load.wait()
-    multiply(0, True, 0, q_tiles - 1)
-    ready(1)
+    multiply(0, True, 0, q_tiles // 2)
+    run(relay, 1)
+    run(collect, 1)
     multiply(1, True)
+    run(forward, 2, 3)
     multiply_kv(1)
-    ready(2, 3)
+    run(relay, 2, 3)
+    run(collect, 2, 3)
     multiply_kv(3)
     multiply(2, False)
+    pass_near(0, [(2, t) for t in range(q_tiles)])
     multiply_kv(2)
     multiply_kv(0)
-    make_tables()
-    pass_near(0, [(2, t) for t in range(q_tiles)])
     multiply(3, False)
-    multiply(0, False, q_tiles - 1)
+    multiply(0, False, q_tiles // 2)
     for c, j in ((2, 0), (0, 1)):
         kv_copy(j).wait_recv()
         own[c, q_tiles] = own[c, q_tiles] + kv_in[j].astype(jnp.float32)
         y_out[c, q_tiles] = own[c, q_tiles, other_rows, :].astype(jnp.bfloat16)
 
+    make_tables()
     y_later = [(2, q_tiles), (0, q_tiles)] + [(3, t) for t in range(q_tiles)]
     for t in range(q_tiles):
         total = pair_sum(2, t)
@@ -291,7 +295,7 @@
     mid_copy(q_tiles).start()
     for later in y_later[q_tiles:]:
         y_copy(*later).start()
-    pass_near(1, [(0, q_tiles - 1)])
+    pass_near(1, [(0, t) for t in range(q_tiles // 2, q_tiles)])
 
     def rope(head):
         return head * cosine[...] + pltpu.roll(head, HEAD_DIM // 2, 1) * sine[...]

time: 80.8 us -> 81.9 us (1.014)
  no operation moved by 1% of the time
where the time goes in v8:
time: 81.9 us; the launch traced here: 81.4 us
  Pallas kernels  79.2 us (97%)
  local copies, waits for them, and re-layouts  2.21 us (3%)
    pallas_call x1, Pallas kernels, attend_on_slice(): pl.pallas_call(attend_kernel, out_shape=jax.ShapeDtypeStruct((pack, query...  79.2 us
    unnamed x5, local copies, waits for them, and re-layouts  2.21 us

profile of v8, /device:TPU:0, one launch (start us, length us, event | category | flops | bytes accessed | tf_op | source)
XLA Modules:
  0.0 81.4 jit_solution(5584852957245660608)
XLA Ops:
  0.0 0.0 copy-start
  0.0 0.8 copy-done
  0.8 0.0 copy-start.1
  0.8 0.7 copy-done.1
  1.4 79.2 %shard_map.64 = bf16[128,2048]{1,0:T(8,128)(2,1)S(1)} custom-call(bf16[32,8192]{1,0:T(8,128)(2,1)} %tokens_ref.1, f32[1,8192]{1,0:T(1,128)S(1)} %bitcast.2, bf16[1024,2048]{1,0:T(8,128)(2,1)} %query_ref.1, bf16[1024,1024]{1,0:T(8,128)(2,1)} %key_ref.1, bf16[1024,1024]{1,0:T(8,128)(2,1)} %value_ref.1, s32[1,128]{1,0:T(1,128)S(1)} %bitcast.3), custom_call_target="tpu_custom_call" | custom-call | flops 5368709120 | bytes 5242880 | tf_op jit(solution)/shard_map/pallas_call | solution.py:362
  80.6 0.8 copy.8
Async XLA Ops:
  0.0 0.8 copy-start
  0.8 0.7 copy-start.1
